TPU v7x, 128 devices: a whole 4x4x4 slice. The times are simulated.
128 devices in a mesh: lat: 8 (over z_lo, y), lon: 16 (over z_hi, x, core).
Axes of the slice: x: 4, y: 4, z: 4 (z_hi: 2, z_lo: 2; z = z_hi * 2 + z_lo), core: 2. Of those that a mesh axis runs over, the one named last changes fastest.
Arguments:
- level_slabs: bfloat16 [8, 96, 768, 512], P('lat', 'lon'), may hold values from -6 to 6
- surf_tokens: bfloat16 [96, 768, 512], P('lat', 'lon'), may hold values from -6 to 6
- level_order: int32 [8], replicated, may hold values from 0 to 7, each once
- level_embed: bfloat16 [8, 512], replicated, may hold values from -6 to 6
- kv_gain: float32 [512], replicated, may hold values from 0.1 to 1.9
- latent_queries: bfloat16 [3, 512], replicated
- w_key: bfloat16 [512, 512], replicated, may hold values from -0.25 to 0.25
- w_value: bfloat16 [512, 512], replicated, may hold values from -0.25 to 0.25
- w_merge: bfloat16 [512, 512], replicated, may hold values from -0.25 to 0.25
- attn_gain: float32 [512], replicated, may hold values from 0.1 to 1.9
- w_qkv: bfloat16 [512, 1536], replicated
- w_out: bfloat16 [512, 512], replicated, may hold values from -0.25 to 0.25
- mlp_gain: float32 [512], replicated, may hold values from 0.1 to 1.9
- w_up: bfloat16 [512, 2048], replicated, may hold values from -0.25 to 0.25
- w_down: bfloat16 [2048, 512], replicated, may hold values from -0.125 to 0.125
- window_shift: int32 [2, 2], replicated, may hold values from 1 to 6, as said below
Outputs:
- blended: bfloat16 [4, 96, 768, 512], P(None, 'lat', 'lon')
Inputs may be any that keep to these rules, and one draw needn't show every extreme that they name: window_shift[b] holds block b's shift along latitude, 1 to 3, and along longitude, 1 to 6; in every draw some block has both at their largest.
All inputs are finite; a program needn't handle non-finite values.
Results may differ from a plain program's by a relative error of at most 0.015.
Values may be sent and summed in bfloat16 or wider, within the bound.
A program may use at most 192 MiB of HBM per device.

v0:
```python
import math

import jax
import jax.numpy as jnp
from jax import lax
from jax.sharding import PartitionSpec as P

HEADS = 16
DEPTH_WIN = 2
WIN_LAT = 6
WIN_LON = 12


def passed_along(value, axis, steps):
    count = lax.axis_size(axis)
    pairs = [(source, (source + steps) % count) for source in range(count)]
    return lax.ppermute(value, axis, pairs)


def layer_norm(values_in, gain_vec):
    row_mean = jnp.mean(values_in, axis=-1, keepdims=True)
    centred = values_in - row_mean
    variance = jnp.mean(centred * centred, axis=-1, keepdims=True)
    return centred * lax.rsqrt(variance + 1e-05) * gain_vec


def perceive(slab_rows, embed_rows, kv_gain, latent_queries, w_key, w_value, w_merge):
    levels, patches, features = slab_rows.shape
    head_size = features // HEADS
    query_count = latent_queries.shape[0]
    tokens = slab_rows.astype(jnp.float32) + embed_rows[:, None, :]
    normed = layer_norm(tokens, kv_gain).astype(jnp.bfloat16).reshape(levels * patches, features)
    key_rows = jnp.dot(normed, w_key, preferred_element_type=jnp.float32).astype(jnp.bfloat16)
    value_rows = jnp.dot(normed, w_value, preferred_element_type=jnp.float32).astype(jnp.bfloat16)
    key_rows = key_rows.reshape(levels, patches, HEADS, head_size)
    value_rows = value_rows.reshape(levels, patches, HEADS, head_size)
    queries = latent_queries.reshape(query_count, HEADS, head_size)
    scores = jnp.einsum(
        "ahe,lnhe->nhal", queries, key_rows, preferred_element_type=jnp.float32
    ) / math.sqrt(head_size)
    weights = jax.nn.softmax(scores, axis=-1).astype(jnp.bfloat16)
    attended = jnp.einsum(
        "nhal,lnhe->anhe", weights, value_rows, preferred_element_type=jnp.float32
    ).astype(jnp.bfloat16)
    attended = attended.reshape(query_count * patches, features)
    merged = jnp.dot(attended, w_merge, preferred_element_type=jnp.float32).reshape(
        query_count, patches, features
    )
    merged = merged + latent_queries.astype(jnp.float32)[:, None, :]
    return merged.astype(jnp.bfloat16)


def to_windows(tensor_in):
    depth, tile_rows, tile_cols = tensor_in.shape[:3]
    rest = tensor_in.shape[3:]
    shaped = tensor_in.reshape(
        (depth, tile_rows // WIN_LAT, WIN_LAT, tile_cols // WIN_LON, WIN_LON) + rest
    )
    moved = shaped.transpose((1, 3, 0, 2, 4) + tuple(range(5, 5 + len(rest))))
    return moved.reshape(
        (tile_rows // WIN_LAT * (tile_cols // WIN_LON), depth * WIN_LAT * WIN_LON) + rest
    )


def from_windows(tensor_in, depth_blocks, grid_lat, grid_lon):
    features = tensor_in.shape[-1]
    shaped = tensor_in.reshape(
        depth_blocks, grid_lat, grid_lon, DEPTH_WIN, WIN_LAT, WIN_LON, features
    )
    moved = shaped.transpose(0, 3, 1, 4, 2, 5, 6)
    return moved.reshape(depth_blocks * DEPTH_WIN, grid_lat * WIN_LAT, grid_lon * WIN_LON, features)


def window_attention(windows, region, attn_gain, w_qkv, w_out):
    batch, span, features = windows.shape
    head_size = features // HEADS
    normed = layer_norm(windows.astype(jnp.float32), attn_gain).astype(jnp.bfloat16)
    projected = jnp.dot(
        normed.reshape(batch * span, features), w_qkv, preferred_element_type=jnp.float32
    )
    projected = projected.astype(jnp.bfloat16).reshape(batch, span, 3, HEADS, head_size)
    scores = jnp.einsum(
        "bqhe,bkhe->bhqk",
        projected[:, :, 0],
        projected[:, :, 1],
        preferred_element_type=jnp.float32,
    ) / math.sqrt(head_size)
    allowed = region[:, :, None] == region[:, None, :]
    scores = jnp.where(allowed[:, None], scores, -1e30)
    weights = jax.nn.softmax(scores, axis=-1).astype(jnp.bfloat16)
    attended = jnp.einsum(
        "bhqk,bkhe->bqhe", weights, projected[:, :, 2], preferred_element_type=jnp.float32
    ).astype(jnp.bfloat16)
    attended = attended.reshape(batch * span, features)
    summed = windows.astype(jnp.float32).reshape(batch * span, features) + jnp.dot(
        attended, w_out, preferred_element_type=jnp.float32
    )
    return summed.astype(jnp.bfloat16).reshape(batch, span, features)


def feed_forward(rows_in, mlp_gain, w_up, w_down):
    normed = layer_norm(rows_in.astype(jnp.float32), mlp_gain).astype(jnp.bfloat16)
    hidden_units = jax.nn.gelu(jnp.dot(normed, w_up, preferred_element_type=jnp.float32)).astype(
        jnp.bfloat16
    )
    summed = rows_in.astype(jnp.float32) + jnp.dot(
        hidden_units, w_down, preferred_element_type=jnp.float32
    )
    return summed.astype(jnp.bfloat16)


def slice_blocks(joined, starts, length, axis_dim):
    depth_blocks = len(starts)
    return jnp.concatenate(
        [
            lax.dynamic_slice_in_dim(
                joined[block_id * DEPTH_WIN : (block_id + 1) * DEPTH_WIN],
                starts[block_id],
                length,
                axis_dim,
            )
            for block_id in range(depth_blocks)
        ],
        0,
    )


def move_back(field, window_shift, depth_blocks):
    tile_rows = field.shape[1]
    tile_cols = field.shape[2]
    sent_back = field
    incoming = passed_along(sent_back, "lon", 1)
    joined = jnp.concatenate([incoming, field], 2)
    starts = [incoming.shape[2] - window_shift[block_id, 1] for block_id in range(depth_blocks)]
    field = slice_blocks(joined, starts, tile_cols, 2)
    sent_back = field
    incoming = passed_along(sent_back, "lat", 1)
    joined = jnp.concatenate([incoming, field], 1)
    starts = [incoming.shape[1] - window_shift[block_id, 0] for block_id in range(depth_blocks)]
    return slice_blocks(joined, starts, tile_rows, 1)


def shards(
    level_slabs,
    surf_tokens,
    level_order,
    level_embed,
    kv_gain,
    latent_queries,
    w_key,
    w_value,
    w_merge,
    attn_gain,
    w_qkv,
    w_out,
    mlp_gain,
    w_up,
    w_down,
    window_shift,
):
    gathered = lax.all_to_all(
        lax.all_to_all(level_slabs, "lon", split_axis=2, concat_axis=1, tiled=True),
        "lat",
        split_axis=1,
        concat_axis=0,
        tiled=True,
    )
    levels, tile_rows, tile_cols, features = gathered.shape
    picker = (level_order[:, None] == jnp.arange(levels, dtype=jnp.int32)[None, :]).astype(
        jnp.float32
    )
    embed_rows = jnp.dot(picker, level_embed.astype(jnp.float32), precision=lax.Precision.HIGHEST)
    atmosphere = perceive(
        gathered.reshape(levels, tile_rows * tile_cols, features),
        embed_rows,
        kv_gain,
        latent_queries,
        w_key,
        w_value,
        w_merge,
    )
    atmosphere = atmosphere.reshape(-1, tile_rows, tile_cols, features)
    latent = jnp.concatenate([surf_tokens[None], atmosphere], 0)
    depth_blocks = latent.shape[0] // DEPTH_WIN
    sent_ahead = latent
    incoming = passed_along(sent_ahead, "lat", -1)
    joined = jnp.concatenate([latent, incoming], 1)
    rolled = slice_blocks(
        joined, [window_shift[block_id, 0] for block_id in range(depth_blocks)], tile_rows, 1
    )
    sent_ahead = rolled
    incoming = passed_along(sent_ahead, "lon", -1)
    joined = jnp.concatenate([rolled, incoming], 2)
    rolled = slice_blocks(
        joined, [window_shift[block_id, 1] for block_id in range(depth_blocks)], tile_cols, 2
    )
    total_rows = tile_rows * lax.axis_size("lat")
    global_rows = lax.axis_index("lat") * tile_rows + jnp.arange(tile_rows, dtype=jnp.int32)
    pieces = []
    regions = []
    for block_id in range(depth_blocks):
        segment = rolled[block_id * DEPTH_WIN : (block_id + 1) * DEPTH_WIN]
        pieces.append(to_windows(segment))
        region = (global_rows >= total_rows - window_shift[block_id, 0]).astype(jnp.int32)
        region_grid = jnp.broadcast_to(
            region[None, :, None, None], (DEPTH_WIN, tile_rows, tile_cols, 1)
        )
        regions.append(to_windows(region_grid)[..., 0])
    windows = jnp.concatenate(pieces, 0)
    region_all = jnp.concatenate(regions, 0)
    attended = window_attention(windows, region_all, attn_gain, w_qkv, w_out)
    first_sum = from_windows(attended, depth_blocks, tile_rows // WIN_LAT, tile_cols // WIN_LON)
    unrolled = move_back(first_sum, window_shift, depth_blocks)
    result = feed_forward(unrolled.reshape(-1, features), mlp_gain, w_up, w_down).reshape(
        unrolled.shape
    )
    return result


def solution(mesh):
    in_specs = (
        P("lat", "lon", None, None),
        P("lat", "lon", None),
        P(),
        P(),
        P(),
        P(),
        P(),
        P(),
        P(),
        P(),
        P(),
        P(),
        P(),
        P(),
        P(),
        P(),
    )
    out_specs = P(None, "lat", "lon", None)
    return jax.shard_map(shards, mesh=mesh, in_specs=in_specs, out_specs=out_specs, check_vma=False)
```

profile of v0, /device:TPU:1, one launch (start us, length us, event | category | flops | bytes accessed | tf_op | source)
XLA Modules:
  0.0 715.2 jit_solution(12763360088252416229)
XLA Ops:
  0.0 5.3 copy.100
  5.3 82.1 %all_to_all.27 = bf16[1,6,768,512]{3,1,0,2:T(8,128)(2,1)S(1)} all-to-all(bf16[1,6,768,512]{3,1,0,2:T(8,128)(2,1)S(1)} %copy.100), channel_id=1, replica_groups=mesh['lat'=8,'lon'=16] {'lon'}, dimensions={2} | all-to-all | bytes 9437184 | tf_op jit(solution)/shard_map/all_to_all | solution.py:162
  91.6 5.0 all-to-all-start.1
  100.3 51.5 %all-to-all-done.1 = bf16[1,96,48,512]{3,2,0,1:T(8,128)(2,1)} async-done(((bf16[1,96,48,512]{3,2,0,1:T(8,128)(2,1)}), bf16[1,96,48,512]{3,2,0,1:T(8,128)(2,1)}, u32[]{:S(2)}, u32[]{:S(2)}) %all-to-all-start.1) | async-done | bytes 4718624 | tf_op jit(solution)/shard_map/all_to_all | solution.py:161
  159.1 4.1 fusion.19
  163.3 4.2 convolution_convert_fusion.1
  167.5 4.2 convolution_convert_fusion.2
  171.7 6.7 copy.104
  178.5 6.7 copy.105
  185.1 9.5 %reshape.199 = bf16[8,576,16,32]{1,0,3,2:T(8,128)(2,1)} reshape(bf16[4608,512]{0,1:T(8,128)(2,1)} %copy.105) | data formatting | bytes 9437184 | tf_op jit(solution)/shard_map/reshape | solution.py:35
  199.8 9.5 %reshape.198 = bf16[8,576,16,32]{1,0,3,2:T(8,128)(2,1)} reshape(bf16[4608,512]{0,1:T(8,128)(2,1)} %copy.104) | data formatting | bytes 9437184 | tf_op jit(solution)/shard_map/reshape | solution.py:36
  209.2 12.9 %copy.109 = bf16[576,16,3,8]{3,2,1,0:T(4,128)(2,1)} copy(bf16[576,16,3,8]{0,2,3,1:T(4,128)(2,1)} %divide_convert_fusion.4) | data formatting | bytes 884736 | tf_op jit(solution)/shard_map/convert_element_type | solution.py:41
  222.1 18.8 %copy.108 = bf16[8,576,16,32]{3,0,2,1:T(8,128)(2,1)} copy(bf16[8,576,16,32]{1,0,3,2:T(8,128)(2,1)} %reshape.198) | data formatting | bytes 9437184 | tf_op jit(solution)/shard_map/reshape | solution.py:36
  240.9 18.2 %convert_bitcast_fusion = bf16[3,576,16,32]{3,0,2,1:T(4,128)(2,1)} fusion(bf16[8,576,16,32]{3,0,2,1:T(8,128)(2,1)} %copy.108, bf16[576,16,3,8]{3,2,1,0:T(4,128)(2,1)} %copy.109), kind=kOutput, calls=%fused_computation.25 | convolution fusion | flops 15040512 | bytes 6930432 | tf_op jit(solution)/shard_map/nhal,lnhe->anhe/dot_general | solution.py:42
  259.2 12.4 %copy.110 = bf16[3,576,16,32]{1,3,2,0:T(8,128)(2,1)} copy(bf16[3,576,16,32]{3,0,2,1:T(4,128)(2,1)} %convert_bitcast_fusion) | data formatting | bytes 3538944 | tf_op jit(solution)/shard_map/convert_element_type | solution.py:44
  277.3 3.9 pad_maximum_fusion.2
  281.1 15.7 %collective-permute-start = (bf16[4,12,48,512]{3,0,2,1:T(4,128)(2,1)}, bf16[4,12,48,512]{3,0,2,1:T(4,128)(2,1)}, u32[]{:S(2)}, u32[]{:S(2)}) collective-permute-start(bf16[4,12,48,512]{3,0,2,1:T(4,128)(2,1)} %pad_maximum_fusion.2), channel_id=1, source_target_pairs={{0,112},{16,0},{32,16},{48,32},{64,48},{80,64},{96,80},{112,96},{1... | collective-permute-start | bytes 7077896 | tf_op jit(solution)/shard_map/ppermute | solution.py:17
  301.6 43.7 %collective-permute-done = bf16[4,12,48,512]{3,0,2,1:T(4,128)(2,1)} collective-permute-done((bf16[4,12,48,512]{3,0,2,1:T(4,128)(2,1)}, bf16[4,12,48,512]{3,0,2,1:T(4,128)(2,1)}, u32[]{:S(2)}, u32[]{:S(2)}) %collective-permute-start) | collective-permute-done | bytes 2359328 | tf_op jit(solution)/shard_map/ppermute | solution.py:17
  345.4 5.9 pad_maximum_fusion
  351.2 7.3 %fusion.60 = (bf16[2,24,48,512]{3,0,2,1:T(2,128)(2,1)}, bf16[2,24,48,512]{3,0,2,1:T(2,128)(2,1)}) fusion(bf16[4,24,48,512]{3,0,2,1:T(4,128)(2,1)S(1)} %pad_maximum_fusion), kind=kLoop, calls=%fused_computation.106 | loop fusion | bytes 9437184 | tf_op jit(solution)/shard_map/slice | solution.py:117
  358.5 3.9 constant_dynamic-slice_fusion.6
  363.4 3.8 pad_maximum_fusion.3
  377.6 22.5 %collective-permute-done.1 = bf16[4,12,48,512]{3,0,2,1:T(4,128)(2,1)} collective-permute-done((bf16[4,12,48,512]{3,0,2,1:T(4,128)(2,1)}, bf16[4,12,48,512]{3,0,2,1:T(4,128)(2,1)}, u32[]{:S(2)}, u32[]{:S(2)}) %collective-permute-start.1) | collective-permute-done | bytes 2359328 | tf_op jit(solution)/shard_map/ppermute | solution.py:17
  400.1 5.0 pad_maximum_fusion.1
  405.0 4.7 fusion.59
  423.8 4.2 maximum_convert_fusion
  429.5 5.1 copy.116
  438.1 5.8 convolution_convert_fusion
  444.0 10.0 %copy.120 = bf16[2304,1536]{0,1:T(8,128)(2,1)} copy(bf16[2304,1536]{1,0:T(8,128)(2,1)} %convolution_convert_fusion) | data formatting | bytes 14155776 | tf_op jit(solution)/shard_map/convert_element_type | solution.py:81
  454.0 23.0 %reshape.206 = bf16[16,144,3,16,32]{1,0,4,3,2:T(8,128)(2,1)} reshape(bf16[2304,1536]{0,1:T(8,128)(2,1)} %copy.120) | data formatting | bytes 14155776 | tf_op jit(solution)/shard_map/reshape | solution.py:81
  476.9 9.1 %fusion.56 = (bf16[16,144,1,16,32]{1,0,4,3,2:T(8,128)(2,1)}, bf16[16,144,1,16,32]{1,0,4,3,2:T(8,128)(2,1)}, bf16[16,144,1,16,32]{1,0,4,3,2:T(8,128)(2,1)}) fusion(bf16[16,144,3,16,32]{1,0,4,3,2:T(8,128)(2,1)} %reshape.206), kind=kLoop, calls=%fused_computation.102 | loop fusion | bytes 14155776 | tf_op jit(solution)/shard_map/slice | solution.py:92
  486.0 20.8 %fusion.63 = (f32[16,16,144]{2,1,0:T(8,128)S(1)}, f32[16,16,144,144]{2,3,1,0:T(8,128)}) fusion(pred[16,144,144]{1,2,0:T(8,128)(4,1)S(1)} %copy-done.9, bf16[16,144,1,16,32]{1,0,4,3,2:T(8,128)(2,1)} %get-tuple-element.6, bf16[16,144,1,16,32]{1,0,4,3,2:T(8,128)(2,1)} %get-tuple-element.7), kind=kOutput, calls=%fused_computation.109 | convolution fusion | flops 360972416 | bytes 26431488 | tf_op jit(solution)/shard_map/sub | solution.py:90
  506.8 15.3 %convert_bitcast_fusion.1 = bf16[16,144,16,32]{1,3,2,0:T(8,128)(2,1)S(1)} fusion(f32[16,16,144,144]{2,3,1,0:T(8,128)} %get-tuple-element.23, f32[16,16,144]{2,1,0:T(8,128)S(1)} %get-tuple-element.22, bf16[16,144,1,16,32]{1,0,4,3,2:T(8,128)(2,1)} %get-tuple-element.5), kind=kOutput, calls=%fused_computation.54 | convolution fusion | flops 351535104 | bytes 26099712 | tf_op jit(solution)/shard_map/bhqk,bkhe->bqhe/dot_general | solution.py:91
  522.0 4.8 copy.125
  526.9 8.0 %reshape.207 = bf16[2304,512]{0,1:T(8,128)(2,1)} reshape(bf16[16,144,16,32]{1,0,3,2:T(8,128)(2,1)} %copy.125) | data formatting | bytes 4718592 | tf_op jit(solution)/shard_map/reshape | solution.py:94
  534.8 6.0 fusion.35
  540.8 4.9 reshape_reshape.3
  545.7 5.7 copy.126
  551.4 6.5 reshape.208
  560.7 23.5 %collective-permute-done.2 = bf16[4,12,48,512]{3,0,2,1:T(4,128)(2,1)} collective-permute-done((bf16[4,12,48,512]{3,0,2,1:T(4,128)(2,1)}, bf16[4,12,48,512]{3,0,2,1:T(4,128)(2,1)}, u32[]{:S(2)}, u32[]{:S(2)}) %collective-permute-start.2) | collective-permute-done | bytes 2359328 | tf_op jit(solution)/shard_map/ppermute | solution.py:17
  587.9 6.9 fusion.58
  607.2 49.3 %collective-permute-done.3 = bf16[4,12,48,512]{3,0,2,1:T(4,128)(2,1)} collective-permute-done((bf16[4,12,48,512]{3,0,2,1:T(4,128)(2,1)}, bf16[4,12,48,512]{3,0,2,1:T(4,128)(2,1)}, u32[]{:S(2)}, u32[]{:S(2)}) %collective-permute-start.3) | collective-permute-done | bytes 2359328 | tf_op jit(solution)/shard_map/ppermute | solution.py:17
  656.5 5.3 maximum_maximum_fusion
  661.8 7.3 %fusion.57 = (bf16[2,24,48,512]{3,0,2,1:T(2,128)(2,1)}, bf16[2,24,48,512]{3,0,2,1:T(2,128)(2,1)}) fusion(bf16[4,24,48,512]{3,0,2,1:T(4,128)(2,1)S(1)} %maximum_maximum_fusion), kind=kLoop, calls=%fused_computation.103 | loop fusion | bytes 9437184 | tf_op jit(solution)/shard_map/slice | solution.py:117
  679.3 5.8 multiply_reduce_fusion.1
  685.1 5.6 maximum_convert_fusion.1
  692.0 3.9 copy.127
  700.4 14.6 %fusion.29 = bf16[2304,512]{1,0:T(8,128)(2,1)} fusion(f32[4,12,48,512]{3,2,1,0:T(8,128)} %copy-done.4, bf16[2048,512]{1,0:T(8,128)(2,1)S(1)} %copy-done, bf16[2304,512]{1,0:T(8,128)(2,1)} %fusion.28, bf16[512,2048]{1,0:T(8,128)(2,1)} %param.29), kind=kOutput, calls=%fused_computation.43 | convolution fusion | flops 9708503040 | bytes 13631488 | tf_op jit(solution)/shard_map/dot_general | solution.py:106
  (106 shorter events, 81.2 us)
Async XLA Ops:
  0.0 700.4 %copy-start = (bf16[2048,512]{1,0:T(8,128)(2,1)S(1)}, bf16[2048,512]{1,0:T(8,128)(2,1)}, u32[]{:S(2)}) copy-start(bf16[2048,512]{1,0:T(8,128)(2,1)} %param.30) | copy-start | bytes 6291460
  91.6 5.0 copy-start.12
  91.6 5.7 copy-start.20
  91.6 5.7 copy-start.21
  91.6 60.2 %all-to-all-start.1 = ((bf16[1,96,48,512]{3,2,0,1:T(8,128)(2,1)}), bf16[1,96,48,512]{3,2,0,1:T(8,128)(2,1)}, u32[]{:S(2)}, u32[]{:S(2)}) async-start(bf16[1,96,48,512]{3,2,0,1:T(8,128)(2,1)} %bitcast.121), calls=%async_computation.1 | async-start | bytes 9437184 | tf_op jit(solution)/shard_map/all_to_all | solution.py:161
  97.5 0.6 copy-start.11
  159.1 4.2 copy-start.18
  163.3 4.2 copy-start.19
  259.1 12.4 %copy-start.13 = (f32[3,512]{1,0:T(4,128)S(1)}, f32[3,512]{1,0:T(4,128)}, u32[]{:S(2)}) copy-start(f32[3,512]{1,0:T(4,128)} %convert_element_type.116) | copy-start | bytes 18436
  274.3 22.6 %copy-start.14 = (s32[2,2]{1,0:T(2,128)S(1)}, s32[2,2]{1,0:T(2,128)}, u32[]{:S(2)}) copy-start(s32[2,2]{1,0:T(2,128)} %param.31) | copy-start | bytes 52
  275.9 1.4 copy-start.2
  281.1 64.2 %collective-permute-start = (bf16[4,12,48,512]{3,0,2,1:T(4,128)(2,1)}, bf16[4,12,48,512]{3,0,2,1:T(4,128)(2,1)}, u32[]{:S(2)}, u32[]{:S(2)}) collective-permute-start(bf16[4,12,48,512]{3,0,2,1:T(4,128)(2,1)} %pad_maximum_fusion.2), channel_id=1, source_target_pairs={{0,112},{16,0},{32,16},{48,32},{64,48},{80,64},{96,80},{112,96},{1... | collective-permute-start | bytes 7077896 | tf_op jit(solution)/shard_map/ppermute | solution.py:17
  362.4 1.0 copy-start.6
  367.3 32.8 %collective-permute-start.1 = (bf16[4,12,48,512]{3,0,2,1:T(4,128)(2,1)}, bf16[4,12,48,512]{3,0,2,1:T(4,128)(2,1)}, u32[]{:S(2)}, u32[]{:S(2)}) collective-permute-start(bf16[4,12,48,512]{3,0,2,1:T(4,128)(2,1)} %pad_maximum_fusion.3), channel_id=1, source_target_pairs={{0,15},{1,0},{2,1},{3,2},{4,3},{5,4},{6,5},{7,6},{8,7},{9,8},{10,9... | collective-permute-start | bytes 7077896 | tf_op jit(solution)/shard_map/ppermute | solution.py:17
  423.8 4.2 copy-start.3
  429.5 7.3 %copy-start.15 = (f32[512]{0:T(512)S(1)}, f32[512]{0:T(512)}, u32[]{:S(2)}) copy-start(f32[512]{0:T(512)} %param.25) | copy-start | bytes 6148
  434.6 2.2 copy-start.1
  436.7 1.4 copy-start.17
  476.9 9.1 %copy-start.9 = (pred[16,144,144]{1,2,0:T(8,128)(4,1)S(1)}, pred[16,144,144]{1,2,0:T(8,128)(4,1)}, u32[]{:S(2)}) copy-start(pred[16,144,144]{1,2,0:T(8,128)(4,1)} %broadcast_compare_fusion) | copy-start | bytes 995332
  526.9 8.0 %copy-start.10 = (bf16[512,512]{1,0:T(8,128)(2,1)S(1)}, bf16[512,512]{1,0:T(8,128)(2,1)}, u32[]{:S(2)}) copy-start(bf16[512,512]{1,0:T(8,128)(2,1)} %param.27) | copy-start | bytes 1572868
  557.9 26.3 %collective-permute-start.2 = (bf16[4,12,48,512]{3,0,2,1:T(4,128)(2,1)}, bf16[4,12,48,512]{3,0,2,1:T(4,128)(2,1)}, u32[]{:S(2)}, u32[]{:S(2)}) collective-permute-start(bf16[4,12,48,512]{3,0,2,1:T(4,128)(2,1)} %reshape.208), channel_id=1, source_target_pairs={{0,1},{1,2},{2,3},{3,4},{4,5},{5,6},{6,7},{7,8},{8,9},{9,10},{10,1... | collective-permute-start | bytes 7077896 | tf_op jit(solution)/shard_map/ppermute | solution.py:17
  560.7 26.1 %copy-start.8 = (bf16[4,12,48,512]{3,0,2,1:T(4,128)(2,1)S(1)}, bf16[4,12,48,512]{3,0,2,1:T(4,128)(2,1)}, u32[]{:S(2)}) copy-start(bf16[4,12,48,512]{3,0,2,1:T(4,128)(2,1)} %reshape.208) | copy-start | bytes 7077892
  599.4 1.0 copy-start.7
  604.3 52.3 %collective-permute-start.3 = (bf16[4,12,48,512]{3,0,2,1:T(4,128)(2,1)}, bf16[4,12,48,512]{3,0,2,1:T(4,128)(2,1)}, u32[]{:S(2)}, u32[]{:S(2)}) collective-permute-start(bf16[4,12,48,512]{3,0,2,1:T(4,128)(2,1)} %pad_maximum_fusion.4), channel_id=1, source_target_pairs={{0,16},{16,32},{32,48},{48,64},{64,80},{80,96},{96,112},{112,0},{1... | collective-permute-start | bytes 7077896 | tf_op jit(solution)/shard_map/ppermute | solution.py:17
  673.6 1.0 copy-start.5
  692.0 6.0 copy-start.16
  695.9 2.1 copy-start.4
where the time goes:
time: 729 us; the launch traced here: 715 us
  local copies, waits for them, and re-layouts  238 us (33%)
  waiting for transfers between devices  191 us (26%)
  matrix products  95.3 us (13%)
  blocking collectives  82.1 us (11%)
  other arithmetic  69.3 us (10%)
  starting transfers between devices  24.4 us (3%)
  between operations  15.5 us (2%)
    ppermute x4, waiting for transfers between devices, passed_along(): return lax.ppermute(value, axis, pairs)  139 us
    all_to_all x1, blocking collectives, shards(): lax.all_to_all(level_slabs, 'lon', split_axis=2, concat_axis=1, tiled=True)  82.1 us
    all_to_all x1, waiting for transfers between devices, shards(): lax.all_to_all(lax.all_to_all(level_slabs, 'lon', split_axis=2, concat_ax...  51.5 us
    reshape x2, local copies, waits for them, and re-layouts, perceive(): value_rows = value_rows.reshape(levels, patches, HEADS, head_size)  28.3 us
    slice x4, local copies, waits for them, and re-layouts, slice_blocks(): joined[block_id * DEPTH_WIN:(block_id + 1) * DEPTH_WIN]  26.2 us
    reshape x1, local copies, waits for them, and re-layouts, window_attention(): projected.astype(jnp.bfloat16).reshape(batch, span, 3, HEADS, head_size)  23 us
    sub x1, matrix products, window_attention(): weights = jax.nn.softmax(scores, axis=-1).astype(jnp.bfloat16)  20.8 us
    ppermute x4, starting transfers between devices, passed_along(): return lax.ppermute(value, axis, pairs)  19.4 us
  transfers between devices with their start and end apart: 5, of which 5 were waited for; matrix products, arithmetic and copies ran while one was open for 1% of the time, Pallas kernels for 0%

commit v1 on v0

v1 whole, which is shorter than its diff:
```python
import functools
import math

import jax
import jax.numpy as jnp
import numpy as np
from jax import lax
from jax.experimental import pallas as pl
from jax.experimental.pallas import tpu as pltpu
from jax.sharding import PartitionSpec as P

D = 512
HEADS = 16
HEAD = D // HEADS
FF = 2048
ATMOS = 3
LATENT = 4
WIN_LAT = 6
WIN_LON = 12
SPAN = 2 * WIN_LAT * WIN_LON
ROWS = 12
COLS = 48
GRP = 16
GROUPS = COLS // GRP
HALO = 3
PATCHES = WIN_LAT * GRP
BATCH = 4 * SPAN
LANES = 128
LOG2E = math.log2(math.e)
MESH = pl.DeviceIdType.MESH
F32 = jnp.float32
BF16 = jnp.bfloat16
BASES = (0, 0, 16, 32)
OFFSETS = (0, 12, 8, 4)


def dot(a, b):
    return jnp.dot(a, b, preferred_element_type=F32)


def norm(x, gain):
    mean = jnp.mean(x, axis=-1, keepdims=True)
    centred = x - mean
    variance = jnp.mean(centred * centred, axis=-1, keepdims=True)
    return (centred * lax.rsqrt(variance + 1e-05) * gain).astype(BF16)


def gelu(x):
    c = math.sqrt(2.0 / math.pi)
    return 0.5 * x * (1.0 + jnp.tanh(x * (c + (c * 0.044715) * (x * x))))


def kernel(
    lats,
    lons,
    order_ref,
    shift_ref,
    slabs,
    surf,
    embed_ref,
    kv_gain_ref,
    queries_ref,
    attn_gain_ref,
    mlp_gain_ref,
    to_cells_ref,
    from_cells_ref,
    w_key,
    w_value,
    w_merge,
    w_qkv,
    w_out,
    w_up,
    w_down,
    out,
    recv,
    latent,
    result,
    from_north,
    from_west,
    from_corner,
    key_v,
    value_v,
    merge_v,
    qkv_v,
    out_v,
    up_v,
    down_v,
    embed_v,
    fold_v,
    value_p,
    merge_p,
    normed_v,
    values_v,
    scores_v,
    mix_v,
    x_v,
    q_v,
    k_v,
    v_v,
    attended_v,
    y_v,
    send_sem,
    recv_sem,
    weight_sem,
    halo_send,
    halo_recv,
    back_send,
    back_recv,
    out_sem,
):
    la = lax.axis_index("lat")
    lo = lax.axis_index("lon")
    north = lax.rem(la + lats - 1, lats)
    south = lax.rem(la + 1, lats)
    west = lax.rem(lo + lons - 1, lons)
    east = lax.rem(lo + 1, lons)
    half = lax.rem(lo, 2)
    dest_lat = lo // 2
    has_self = dest_lat == la

    def is_self(lat, lon):
        return jnp.logical_and(lat == la, lon == lo)

    barrier = pltpu.get_barrier_semaphore()

    def greet(lat, lon):
        pl.semaphore_signal(barrier, inc=1, device_id=(lat, lon), device_id_type=MESH)

    for lat in range(lats):
        for r in range(2):
            lon = 2 * la + r

            @pl.when(jnp.logical_not(is_self(lat, lon)))
            def _():
                greet(lat, lon)

    for lat, lon in ((south, lo), (la, east), (south, east), (north, lo), (la, west), (north, west)):
        greet(lat, lon)
    pl.semaphore_wait(barrier, 6 + 2 * lats - jnp.where(has_self, 1, 0))

    def part_copy(g, k):
        lon = lax.rem(2 * la + half + k, lons)
        source = slabs.at[0, :, pl.ds(pl.multiple_of(lon * COLS + g * GRP, GRP), GRP), :]
        target = recv.at[g, half, la]
        return lon, source, target

    def send(i, carry):
        g, k = i // lons, lax.rem(i, lons)
        lon, source, target = part_copy(g, k)

        @pl.when(is_self(dest_lat, lon))
        def _():
            pltpu.make_async_copy(source, target, recv_sem.at[g, half, la]).start()

        @pl.when(jnp.logical_not(is_self(dest_lat, lon)))
        def _():
            pltpu.make_async_remote_copy(
                source,
                target,
                send_sem.at[g, k],
                recv_sem.at[g, half, la],
                device_id=(dest_lat, lon),
                device_id_type=MESH,
            ).start()

        return carry

    lax.fori_loop(0, GROUPS * lons, send, 0)

    loads = [
        pltpu.make_async_copy(source, target, weight_sem.at[i])
        for i, (source, target) in enumerate(
            (
                (w_key, key_v),
                (w_value, value_v),
                (w_merge, merge_v),
                (w_qkv, qkv_v),
                (w_out, out_v),
                (w_up, up_v),
                (w_down, down_v),
                (surf, latent.at[0, pl.ds(0, ROWS), pl.ds(0, COLS), :]),
            )
        )
    ]
    for load in loads:
        load.start()
    result[...] = jnp.zeros_like(result)
    embed_v[...] = embed_ref[...].astype(F32)

    new = lax.broadcasted_iota(jnp.int32, (D, D), 1)
    old = lax.broadcasted_iota(jnp.int32, (D, D), 0)
    loads[1].wait()
    value_p[...] = dot(
        value_v[...], jnp.where(old == (new % HEADS) * HEAD + new // HEADS, 1.0, 0.0).astype(BF16)
    ).astype(BF16)
    loads[2].wait()
    merge_p[...] = dot(
        jnp.where(new == (old % HEADS) * HEAD + old // HEADS, 1.0, 0.0).astype(BF16), merge_v[...]
    ).astype(BF16)
    loads[0].wait()
    head_of = lax.broadcasted_iota(jnp.int32, (LANES, D), 1) // HEAD
    row_head = lax.broadcasted_iota(jnp.int32, (LANES, D), 0) % HEADS
    for a in range(ATMOS):
        picked = jnp.where(head_of == row_head, queries_ref[a : a + 1, :].astype(F32), 0.0).astype(BF16)
        folded = lax.dot_general(
            picked, key_v[...], (((1,), (1,)), ((), ())), preferred_element_type=F32
        )
        folded = folded.T * (LOG2E / math.sqrt(HEAD))
        high = folded.astype(BF16)
        fold_v[:, a * LANES : (a + 1) * LANES] = high
        fold_v[:, (ATMOS + a) * LANES : (ATMOS + a + 1) * LANES] = (folded - high.astype(F32)).astype(BF16)

    def aggregate(g, h):
        def one_level(j, carry):
            landed = recv.at[g, h, j]
            pltpu.make_async_copy(landed, landed, recv_sem.at[g, h, j]).wait()
            row = embed_v[pl.ds(order_ref[j], 1), :]
            x = landed[...].reshape(PATCHES, D).astype(F32) + row
            normed_v[pl.ds(pl.multiple_of(j * PATCHES, PATCHES), PATCHES), :] = norm(x, kv_gain_ref[...])
            return carry

        lax.fori_loop(0, lats, one_level, 0)
        values_v[...] = dot(normed_v[...], value_p[...]).astype(BF16)
        scores_v[...] = dot(normed_v[...], fold_v[:, : ATMOS * LANES]) + dot(
            normed_v[...], fold_v[:, ATMOS * LANES :]
        )
        for a in range(ATMOS):
            cut = slice(a * LANES, (a + 1) * LANES)
            level = [scores_v[j * PATCHES : (j + 1) * PATCHES, cut] for j in range(lats)]
            top = functools.reduce(jnp.maximum, level)
            level = [jnp.exp2(s - top) for s in level]
            scale = 1.0 / functools.reduce(jnp.add, level)
            level = [e * scale for e in level]
            for c in range(D // LANES):
                lanes = slice(c * LANES, (c + 1) * LANES)
                mixed = functools.reduce(
                    jnp.add,
                    [
                        level[j] * values_v[j * PATCHES : (j + 1) * PATCHES, lanes].astype(F32)
                        for j in range(lats)
                    ],
                )
                mix_v[a * PATCHES : (a + 1) * PATCHES, lanes] = mixed.astype(BF16)
        merged = dot(mix_v[...], merge_p[...])
        for a in range(ATMOS):
            tokens = merged[a * PATCHES : (a + 1) * PATCHES] + queries_ref[a : a + 1, :].astype(F32)
            latent[
                1 + a, pl.ds(pl.multiple_of(h * WIN_LAT, WIN_LAT), WIN_LAT), g * GRP : (g + 1) * GRP, :
            ] = tokens.astype(BF16).reshape(WIN_LAT, GRP, D)

    def aggregate_group(g):
        lax.fori_loop(0, 2, lambda h, carry: (aggregate(g, h), carry)[1], 0)

    def halo(i, rows, cols, to_rows, to_cols, lat, lon):
        return pltpu.make_async_remote_copy(
            latent.at[:, pl.ds(rows, to_rows[1]), pl.ds(cols, GRP), :],
            latent.at[:, pl.ds(to_rows[0], to_rows[1]), pl.ds(to_cols, GRP), :],
            halo_send.at[i],
            halo_recv.at[i],
            device_id=(lat, lon),
            device_id_type=MESH,
        )

    row_halos = [
        halo(g, 0, g * GRP, (ROWS, HALO), g * GRP, north, lo) for g in range(GROUPS)
    ]
    col_halo = halo(GROUPS, 0, 0, (0, ROWS), COLS, la, west)
    corner_halo = halo(GROUPS + 1, 0, 0, (ROWS, HALO), COLS, north, west)

    last = la == lats - 1

    def attend(pair, rw):
        first_row = rw * WIN_LAT + 1
        windows = [(b, 2 * pair + c) for b in range(2) for c in range(2)]
        for w, (b, cw) in enumerate(windows):
            place = (shift_ref[b, 0] - 1) * 32 + shift_ref[b, 1] + OFFSETS[cw]
            cells = latent[2 * b : 2 * b + 2, pl.ds(first_row, 8), BASES[cw] : BASES[cw] + 32, :]
            at = lax.broadcasted_iota(jnp.int32, (SPAN, 512), 1)
            pick = jnp.where(at == to_cells_ref[...] + place, 1.0, 0.0).astype(BF16)
            x_v[w * SPAN : (w + 1) * SPAN, :] = dot(pick, cells.reshape(512, D))
        normed = norm(x_v[...], attn_gain_ref[...])
        q_v[...] = (dot(normed, qkv_v[:, :D]) * (LOG2E / math.sqrt(HEAD))).astype(BF16)
        k_v[...] = dot(normed, qkv_v[:, D : 2 * D]).astype(BF16)
        v_v[...] = dot(normed, qkv_v[:, 2 * D :]).astype(BF16)
        lane_head = lax.broadcasted_iota(jnp.int32, (SPAN, LANES), 1) // HEAD
        ones = jnp.ones((SPAN, LANES), BF16)
        row_of_q = lax.broadcasted_iota(jnp.int32, (SPAN, SPAN), 0)
        row_of_k = lax.broadcasted_iota(jnp.int32, (SPAN, SPAN), 1)
        row_of_q = (row_of_q // WIN_LON) % WIN_LAT
        row_of_k = (row_of_k // WIN_LON) % WIN_LAT
        edge = jnp.where(jnp.logical_and(last, rw == 1), 0, WIN_LAT)

        def window(w, carry):
            at = pl.ds(pl.multiple_of(w * SPAN, 16), SPAN)
            start = WIN_LAT - shift_ref[w // 2, 0] + edge
            bias = jnp.where((row_of_q >= start) == (row_of_k >= start), 0.0, -1e30)
            for c in range(D // LANES):
                lanes = slice(c * LANES, (c + 1) * LANES)
                q = q_v[at, lanes]
                k = k_v[at, lanes]
                v = jnp.concatenate([v_v[at, lanes], ones], axis=1)
                mixed = jnp.zeros((SPAN, LANES), F32)
                for h in range(LANES // HEAD):
                    own = lane_head == h
                    s = lax.dot_general(
                        jnp.where(own, q, jnp.zeros_like(q)),
                        k,
                        (((1,), (1,)), ((), ())),
                        preferred_element_type=F32,
                    )
                    s = s + bias
                    p = jnp.exp2(s - jnp.max(s, axis=-1, keepdims=True)).astype(BF16)
                    o = dot(p, v)
                    mixed = jnp.where(own, o[:, :LANES] / o[:, LANES:], mixed)
                attended_v[at, lanes] = mixed.astype(BF16)
            return carry

        lax.fori_loop(0, 4, window, 0)
        first = (x_v[...] + dot(attended_v[...], out_v[...])).astype(BF16).astype(F32)
        normed = norm(first, mlp_gain_ref[...])
        total = first
        for c in range(FF // 512):
            cut = slice(c * 512, (c + 1) * 512)
            hidden = gelu(dot(normed, up_v[:, cut])).astype(BF16)
            total = total + dot(hidden, down_v[cut, :])
        y_v[...] = total.astype(BF16)
        for w, (b, cw) in enumerate(windows):
            place = (shift_ref[b, 0] - 1) * 32 + shift_ref[b, 1] + OFFSETS[cw]
            at = lax.broadcasted_iota(jnp.int32, (512, SPAN), 0)
            put = jnp.where(at == from_cells_ref[0:1, :] + place, 1.0, 0.0).astype(BF16)
            moved = dot(put, y_v[w * SPAN : (w + 1) * SPAN, :]).astype(BF16).reshape(2, 8, 32, D)
            where = (slice(2 * b, 2 * b + 2), pl.ds(first_row, 8), slice(BASES[cw], BASES[cw] + 32))
            result[where] = result[where] + moved

    def back(i, source, target, lat, lon):
        return pltpu.make_async_remote_copy(
            source, target, back_send.at[i], back_recv.at[i], device_id=(lat, lon), device_id_type=MESH
        )

    backs = (
        back(0, result.at[:, pl.ds(ROWS, HALO), pl.ds(0, COLS), :], from_north, south, lo),
        back(1, result.at[:, pl.ds(0, ROWS), pl.ds(COLS, GRP), :], from_west, la, east),
        back(2, result.at[:, pl.ds(ROWS, HALO), pl.ds(COLS, GRP), :], from_corner, south, east),
    )

    aggregate_group(0)
    loads[7].wait()
    row_halos[0].start()
    col_halo.start()
    corner_halo.start()
    aggregate_group(1)
    row_halos[1].start()
    for i in range(3, 7):
        loads[i].wait()

    def first_pair(rw, carry):
        @pl.when(rw == 1)
        def _():
            row_halos[0].wait_recv()
            row_halos[1].wait_recv()

        attend(0, rw)
        return carry

    lax.fori_loop(0, 2, first_pair, 0)
    aggregate_group(2)
    row_halos[2].start()

    def second_pair(rw, carry):
        @pl.when(rw == 0)
        def _():
            col_halo.wait_recv()

        @pl.when(rw == 1)
        def _():
            row_halos[2].wait_recv()
            corner_halo.wait_recv()

        attend(1, rw)
        return carry

    lax.fori_loop(0, 2, second_pair, 0)
    for copy in backs:
        copy.start()
    for copy in backs:
        copy.wait_recv()
    result[:, 0:HALO, 0:COLS, :] = result[:, 0:HALO, 0:COLS, :] + from_north[...]
    result[:, 0:ROWS, 0:GRP, :] = result[:, 0:ROWS, 0:GRP, :] + from_west[...]
    result[:, 0:HALO, 0:GRP, :] = result[:, 0:HALO, 0:GRP, :] + from_corner[...]
    done = pltpu.make_async_copy(result.at[:, pl.ds(0, ROWS), pl.ds(0, COLS), :], out, out_sem)
    done.start()
    for copy in backs:
        copy.wait_send()
    for copy in row_halos + [col_halo, corner_halo]:
        copy.wait_send()

    def sent(i, carry):
        g, k = i // lons, lax.rem(i, lons)
        lon, source, target = part_copy(g, k)

        @pl.when(jnp.logical_not(is_self(dest_lat, lon)))
        def _():
            pltpu.make_async_remote_copy(
                source,
                target,
                send_sem.at[g, k],
                recv_sem.at[g, half, la],
                device_id=(dest_lat, lon),
                device_id_type=MESH,
            ).wait_send()

        return carry

    lax.fori_loop(0, GROUPS * lons, sent, 0)
    done.wait()


def shards(
    lats,
    lons,
    level_slabs,
    surf_tokens,
    level_order,
    level_embed,
    kv_gain,
    latent_queries,
    w_key,
    w_value,
    w_merge,
    attn_gain,
    w_qkv,
    w_out,
    mlp_gain,
    w_up,
    w_down,
    window_shift,
):
    token = np.arange(SPAN)
    cell = (token // 72) * 256 + (token % 72) // 12 * 32 + token % 12
    to_cells = jnp.asarray(cell[:, None], jnp.int32)
    from_cells = jnp.asarray(np.broadcast_to(cell[None, :], (8, SPAN)), jnp.int32)
    smem = pl.BlockSpec(memory_space=pltpu.SMEM)
    vmem = pl.BlockSpec(memory_space=pltpu.VMEM)
    hbm = pl.BlockSpec(memory_space=pl.ANY)
    tokens = lats * PATCHES
    return pl.pallas_call(
        functools.partial(kernel, lats, lons),
        out_shape=jax.ShapeDtypeStruct((LATENT, ROWS, COLS, D), BF16),
        in_specs=[smem] * 2 + [hbm] * 2 + [vmem] * 7 + [hbm] * 7,
        out_specs=hbm,
        scratch_shapes=[
            pltpu.VMEM((GROUPS, 2, lats, WIN_LAT, GRP, D), BF16),
            pltpu.VMEM((LATENT, ROWS + HALO, COLS + GRP, D), BF16),
            pltpu.VMEM((LATENT, ROWS + HALO, COLS + GRP, D), BF16),
            pltpu.VMEM((LATENT, HALO, COLS, D), BF16),
            pltpu.VMEM((LATENT, ROWS, GRP, D), BF16),
            pltpu.VMEM((LATENT, HALO, GRP, D), BF16),
            pltpu.VMEM((D, D), BF16),
            pltpu.VMEM((D, D), BF16),
            pltpu.VMEM((D, D), BF16),
            pltpu.VMEM((D, 3 * D), BF16),
            pltpu.VMEM((D, D), BF16),
            pltpu.VMEM((D, FF), BF16),
            pltpu.VMEM((FF, D), BF16),
            pltpu.VMEM((lats, D), F32),
            pltpu.VMEM((D, 2 * ATMOS * LANES), BF16),
            pltpu.VMEM((D, D), BF16),
            pltpu.VMEM((D, D), BF16),
            pltpu.VMEM((tokens, D), BF16),
            pltpu.VMEM((tokens, D), BF16),
            pltpu.VMEM((tokens, ATMOS * LANES), F32),
            pltpu.VMEM((ATMOS * PATCHES, D), BF16),
            pltpu.VMEM((BATCH, D), F32),
            pltpu.VMEM((BATCH, D), BF16),
            pltpu.VMEM((BATCH, D), BF16),
            pltpu.VMEM((BATCH, D), BF16),
            pltpu.VMEM((BATCH, D), BF16),
            pltpu.VMEM((BATCH, D), BF16),
            pltpu.SemaphoreType.DMA((GROUPS, lons)),
            pltpu.SemaphoreType.DMA((GROUPS, 2, lats)),
            pltpu.SemaphoreType.DMA((8,)),
            pltpu.SemaphoreType.DMA((GROUPS + 2,)),
            pltpu.SemaphoreType.DMA((GROUPS + 2,)),
            pltpu.SemaphoreType.DMA((3,)),
            pltpu.SemaphoreType.DMA((3,)),
            pltpu.SemaphoreType.DMA,
        ],
        compiler_params=pltpu.CompilerParams(
            collective_id=0, has_side_effects=True, vmem_limit_bytes=56 * 1024 * 1024
        ),
        name="encoder",
    )(
        level_order,
        window_shift,
        level_slabs,
        surf_tokens,
        level_embed,
        kv_gain.reshape(1, D),
        latent_queries,
        attn_gain.reshape(1, D),
        mlp_gain.reshape(1, D),
        to_cells,
        from_cells,
        w_key,
        w_value,
        w_merge,
        w_qkv,
        w_out,
        w_up,
        w_down,
    )


def solution(mesh):
    in_specs = (P("lat", "lon", None, None), P("lat", "lon", None)) + (P(),) * 14
    return jax.shard_map(
        functools.partial(shards, mesh.shape["lat"], mesh.shape["lon"]),
        mesh=mesh,
        in_specs=in_specs,
        out_specs=P(None, "lat", "lon", None),
        check_vma=False,
    )
```

time: 729 us -> 195 us (0.27); the launches traced: 715 us -> 195 us
  local copies, waits for them, and re-layouts: 238 us -> 3.24 us
  Pallas kernels: 0 us -> 192 us
  waiting for transfers between devices: 191 us -> 0 us
  matrix products: 95.3 us -> 0 us
  blocking collectives: 82.1 us -> 0 us
  other arithmetic: 69.3 us -> 0 us
  starting transfers between devices: 24.4 us -> 0 us
  between operations: 15.5 us -> 0.01 us
    pallas_call x0 -> x1, Pallas kernels: none -> 192 us  [shards(): pl.pallas_call(functools.partial(kernel, lats, lons), out_shape=jax.Shape...]
    ppermute x4 -> x0, waiting for transfers between devices: 139 us -> none  [passed_along(): return lax.ppermute(value, axis, pairs)]
    reshape x10 -> x0, local copies, waits for them, and re-layouts: 82.3 us -> none  [the longest x2 28.3 us: perceive(): value_rows = value_rows.reshape(levels, patches, HEADS, head_size)]
    all_to_all x1 -> x0, blocking collectives: 82.1 us -> none  [shards(): lax.all_to_all(level_slabs, 'lon', split_axis=2, concat_axis=1, tiled=True)]
    dot_general x10 -> x0, matrix products: 74.6 us -> none  [the longest x1 18.2 us: perceive(): jnp.einsum('nhal,lnhe->anhe', weights, value_rows, preferred_element_type...]
    convert_element_type x8 -> x0, local copies, waits for them, and re-layouts: 62.5 us -> none  [the longest x1 12.9 us: perceive(): weights = jax.nn.softmax(scores, axis=-1).astype(jnp.bfloat16)]
    all_to_all x1 -> x0, waiting for transfers between devices: 51.5 us -> none  [shards(): lax.all_to_all(lax.all_to_all(level_slabs, 'lon', split_axis=2, concat_ax...]
    slice x6 -> x0, local copies, waits for them, and re-layouts: 35.9 us -> none  [the longest x4 26.2 us: slice_blocks(): joined[block_id * DEPTH_WIN:(block_id + 1) * DEPTH_WIN]]
  transfers between devices with their start and end apart: 5 -> 0, of which waited for: 5 -> 0; matrix products, arithmetic and copies ran while one was open for 1% -> 0% of each run, Pallas kernels for 0% -> 0%
where the time goes in v1:
time: 195 us
  Pallas kernels  192 us (98%)
  local copies, waits for them, and re-layouts  3.24 us (2%)
    pallas_call x1, Pallas kernels, shards(): pl.pallas_call(functools.partial(kernel, lats, lons), out_shape=jax.Shape...  192 us

profile of v1, /device:TPU:1, one launch (start us, length us, event | category | flops | bytes accessed | tf_op | source)
XLA Modules:
  0.0 195.2 jit_solution(10231192627045221997)
XLA Ops:
  0.0 192.0 %encoder.1 = bf16[4,12,48,512]{3,2,1,0:T(8,128)(2,1)} custom-call(s32[8]{0:T(128)} %order_ref.1, s32[2,2]{1,0:T(2,128)} %shift_ref.1, bf16[1,6,768,512]{3,2,1,0:T(8,128)(2,1)} %slabs.1, bf16[12,48,512]{2,1,0:T(8,128)(2,1)} %surf.1, bf16[8,512]{1,0:T(8,128)(2,1)} %embed_ref.1, f32[1,512]{1,0:T(1,128)} %bitcast.3, bf16[3,512]{1,0:T(4,128)(2,1)} %queries_ref.1, ...), custom_call_target="tpu_custom_call" | custom-call | tf_op jit(solution)/shard_map/encoder/pallas_call | solution.py:446
  192.0 3.2 %copy.20 = bf16[4,12,48,512]{3,2,1,0:T(8,128)(2,1)} copy(bf16[4,12,48,512]{3,2,1,0:T(8,128)(2,1)} %encoder.1) | data formatting | bytes 4718592

commit v2 on v1

--- a/solution.py
+++ b/solution.py
@@ -23,8 +23,9 @@
 GRP = 16
 GROUPS = COLS // GRP
 HALO = 3
+EDGE = 8
 PATCHES = WIN_LAT * GRP
-BATCH = 4 * SPAN
+BATCH = 2 * SPAN
 LANES = 128
 LOG2E = math.log2(math.e)
 MESH = pl.DeviceIdType.MESH
@@ -73,11 +74,16 @@
     w_down,
     out,
     recv,
+    relay,
     latent,
     result,
     from_north,
     from_west,
     from_corner,
+    ahead_out,
+    ahead_in,
+    ahead_corner,
+    back_out,
     key_v,
     value_v,
     merge_v,
@@ -101,6 +107,8 @@
     y_v,
     send_sem,
     recv_sem,
+    relay_send,
+    relay_recv,
     weight_sem,
     halo_send,
     halo_recv,
@@ -117,6 +125,10 @@
     half = lax.rem(lo, 2)
     dest_lat = lo // 2
     has_self = dest_lat == la
+    half_lats, half_lons = lats // 2, lons // 2
+    z_lo, z_hi = la // half_lats, lo // half_lons
+    outer = z_lo == z_hi
+    across = lax.rem(la + half_lats, lats)
 
     def is_self(lat, lon):
         return jnp.logical_and(lat == la, lon == lo)
@@ -129,31 +141,41 @@
     for lat in range(lats):
         for r in range(2):
             lon = 2 * la + r
-
-            @pl.when(jnp.logical_not(is_self(lat, lon)))
+            by_relay = jnp.logical_and(jnp.logical_not(outer), lat // half_lats == z_lo)
+
+            @pl.when(jnp.logical_not(jnp.logical_or(is_self(lat, lon), by_relay)))
             def _():
                 greet(lat, lon)
 
+    @pl.when(jnp.logical_not(outer))
+    def _():
+        greet(across, lo)
+
+    @pl.when(outer)
+    def _():
+        for y in range(half_lats):
+            for r in range(2):
+                greet((1 - z_lo) * half_lats + y, 2 * across + r)
+
     for lat, lon in ((south, lo), (la, east), (south, east), (north, lo), (la, west), (north, west)):
         greet(lat, lon)
-    pl.semaphore_wait(barrier, 6 + 2 * lats - jnp.where(has_self, 1, 0))
-
-    def part_copy(g, k):
-        lon = lax.rem(2 * la + half + k, lons)
+    pl.semaphore_wait(barrier, 6 + 2 * lats + jnp.where(outer, 1, 0) - jnp.where(has_self, 1, 0))
+
+    def part_to(k):
+        x = lax.rem(lax.rem(lo, half_lons) // 2 + k, half_lats)
+        core = lax.rem(half + k // half_lons, 2)
+        return lax.rem(z_hi + 1 + k // half_lats, 2) * half_lons + 2 * x + core
+
+    def relayed(lon):
+        return jnp.logical_and(outer, lon // half_lons != z_hi)
+
+    def part_copies(g, k):
+        lon = part_to(k)
         source = slabs.at[0, :, pl.ds(pl.multiple_of(lon * COLS + g * GRP, GRP), GRP), :]
         target = recv.at[g, half, la]
-        return lon, source, target
-
-    def send(i, carry):
-        g, k = i // lons, lax.rem(i, lons)
-        lon, source, target = part_copy(g, k)
-
-        @pl.when(is_self(dest_lat, lon))
-        def _():
-            pltpu.make_async_copy(source, target, recv_sem.at[g, half, la]).start()
-
-        @pl.when(jnp.logical_not(is_self(dest_lat, lon)))
-        def _():
+        y = lax.rem(la, half_lats)
+        return (
+            pltpu.make_async_copy(source, target, recv_sem.at[g, half, la]),
             pltpu.make_async_remote_copy(
                 source,
                 target,
@@ -161,11 +183,78 @@
                 recv_sem.at[g, half, la],
                 device_id=(dest_lat, lon),
                 device_id_type=MESH,
-            ).start()
-
+            ),
+            pltpu.make_async_remote_copy(
+                source,
+                relay.at[g, half, y],
+                send_sem.at[g, k],
+                relay_recv.at[g, half, y],
+                device_id=(lax.rem(dest_lat + half_lats, lats), lon),
+                device_id_type=MESH,
+            ),
+        )
+
+    def send_part(g, k):
+        lon = part_to(k)
+        own = is_self(dest_lat, lon)
+
+        @pl.when(own)
+        def _():
+            part_copies(g, k)[0].start()
+
+        @pl.when(relayed(lon))
+        def _():
+            part_copies(g, k)[2].start()
+
+        @pl.when(jnp.logical_not(jnp.logical_or(own, relayed(lon))))
+        def _():
+            part_copies(g, k)[1].start()
+
+    def sent_part(g, k):
+        @pl.when(jnp.logical_not(is_self(dest_lat, part_to(k))))
+        def _():
+            part_copies(g, k)[1].wait_send()
+
+    def relay_copy(g, h, y):
+        level = (1 - z_lo) * half_lats + y
+        return pltpu.make_async_remote_copy(
+            relay.at[g, h, y],
+            recv.at[g, h, level],
+            relay_send.at[g, h, y],
+            recv_sem.at[g, h, level],
+            device_id=(across, lo),
+            device_id_type=MESH,
+        )
+
+    def send_on(g, first):
+        @pl.when(outer)
+        def _():
+            h = half if first else 1 - half
+
+            def step(y, carry):
+                landed = relay.at[g, h, y]
+                pltpu.make_async_copy(landed, landed, relay_recv.at[g, h, y]).wait()
+                relay_copy(g, h, y).start()
+                return carry
+
+            lax.fori_loop(0, half_lats, step, 0)
+
+    def next_group(g):
+        def step(k, carry):
+            sent_part(g, k)
+            send_part(g + 1, k)
+            return carry
+
+        lax.fori_loop(0, lons // 2, step, 0)
+        send_on(g, True)
+        lax.fori_loop(lons // 2, lons, step, 0)
+        send_on(g, False)
+
+    def first_part(k, carry):
+        send_part(0, k)
         return carry
 
-    lax.fori_loop(0, GROUPS * lons, send, 0)
+    lax.fori_loop(0, lons, first_part, 0)
 
     loads = [
         pltpu.make_async_copy(source, target, weight_sem.at[i])
@@ -185,6 +274,7 @@
     for load in loads:
         load.start()
     result[...] = jnp.zeros_like(result)
+    latent[:, :, COLS : COLS + GRP, :] = jnp.zeros((LATENT, ROWS + HALO, GRP, D), BF16)
     embed_v[...] = embed_ref[...].astype(F32)
 
     new = lax.broadcasted_iota(jnp.int32, (D, D), 1)
@@ -251,30 +341,54 @@
     def aggregate_group(g):
         lax.fori_loop(0, 2, lambda h, carry: (aggregate(g, h), carry)[1], 0)
 
-    def halo(i, rows, cols, to_rows, to_cols, lat, lon):
+    def halo(i, levels, rows, cols, to_row, to_col, lat, lon):
         return pltpu.make_async_remote_copy(
-            latent.at[:, pl.ds(rows, to_rows[1]), pl.ds(cols, GRP), :],
-            latent.at[:, pl.ds(to_rows[0], to_rows[1]), pl.ds(to_cols, GRP), :],
+            latent.at[pl.ds(*levels), pl.ds(0, rows), pl.ds(cols, GRP), :],
+            latent.at[pl.ds(*levels), pl.ds(to_row, rows), pl.ds(to_col, GRP), :],
             halo_send.at[i],
             halo_recv.at[i],
             device_id=(lat, lon),
             device_id_type=MESH,
         )
 
+    every = (0, LATENT)
     row_halos = [
-        halo(g, 0, g * GRP, (ROWS, HALO), g * GRP, north, lo) for g in range(GROUPS)
+        halo(0, every, HALO, 0, ROWS, 0, north, lo),
+        halo(1, every, HALO, GRP, ROWS, GRP, north, lo),
+        halo(2, (0, 2), HALO, 2 * GRP, ROWS, 2 * GRP, north, lo),
+        halo(3, (2, 2), HALO, 2 * GRP, ROWS, 2 * GRP, north, lo),
     ]
-    col_halo = halo(GROUPS, 0, 0, (0, ROWS), COLS, la, west)
-    corner_halo = halo(GROUPS + 1, 0, 0, (ROWS, HALO), COLS, north, west)
+
+    def packed(cells):
+        levels, rows = cells.shape[:2]
+        return cells.astype(F32).reshape(levels, rows // 2, GRP, D).astype(BF16)
+
+    def unpacked(cells):
+        levels, pairs = cells.shape[:2]
+        return cells.astype(F32).reshape(levels, 2 * pairs, EDGE, D).astype(BF16)
+
+    col_halo = pltpu.make_async_remote_copy(
+        ahead_out, ahead_in, halo_send.at[4], halo_recv.at[4], device_id=(la, west), device_id_type=MESH
+    )
+    corner_halo = pltpu.make_async_remote_copy(
+        ahead_out.at[:, pl.ds(0, 2), :, :],
+        ahead_corner,
+        halo_send.at[5],
+        halo_recv.at[5],
+        device_id=(north, west),
+        device_id_type=MESH,
+    )
 
     last = la == lats - 1
 
-    def attend(pair, rw):
+    def attend(pair, rw, b):
         first_row = rw * WIN_LAT + 1
-        windows = [(b, 2 * pair + c) for b in range(2) for c in range(2)]
-        for w, (b, cw) in enumerate(windows):
-            place = (shift_ref[b, 0] - 1) * 32 + shift_ref[b, 1] + OFFSETS[cw]
-            cells = latent[2 * b : 2 * b + 2, pl.ds(first_row, 8), BASES[cw] : BASES[cw] + 32, :]
+        s, t = shift_ref[b, 0], shift_ref[b, 1]
+        levels = pl.ds(2 * b, 2)
+        columns = (2 * pair, 2 * pair + 1)
+        for w, cw in enumerate(columns):
+            place = (s - 1) * 32 + t + OFFSETS[cw]
+            cells = latent[levels, pl.ds(first_row, 8), BASES[cw] : BASES[cw] + 32, :]
             at = lax.broadcasted_iota(jnp.int32, (SPAN, 512), 1)
             pick = jnp.where(at == to_cells_ref[...] + place, 1.0, 0.0).astype(BF16)
             x_v[w * SPAN : (w + 1) * SPAN, :] = dot(pick, cells.reshape(512, D))
@@ -288,11 +402,10 @@
         row_of_k = lax.broadcasted_iota(jnp.int32, (SPAN, SPAN), 1)
         row_of_q = (row_of_q // WIN_LON) % WIN_LAT
         row_of_k = (row_of_k // WIN_LON) % WIN_LAT
-        edge = jnp.where(jnp.logical_and(last, rw == 1), 0, WIN_LAT)
+        start = WIN_LAT - s + jnp.where(jnp.logical_and(last, rw == 1), 0, WIN_LAT)
 
         def window(w, carry):
             at = pl.ds(pl.multiple_of(w * SPAN, 16), SPAN)
-            start = WIN_LAT - shift_ref[w // 2, 0] + edge
             bias = jnp.where((row_of_q >= start) == (row_of_k >= start), 0.0, -1e30)
             for c in range(D // LANES):
                 lanes = slice(c * LANES, (c + 1) * LANES)
@@ -315,7 +428,7 @@
                 attended_v[at, lanes] = mixed.astype(BF16)
             return carry
 
-        lax.fori_loop(0, 4, window, 0)
+        lax.fori_loop(0, 2, window, 0)
         first = (x_v[...] + dot(attended_v[...], out_v[...])).astype(BF16).astype(F32)
         normed = norm(first, mlp_gain_ref[...])
         total = first
@@ -324,12 +437,12 @@
             hidden = gelu(dot(normed, up_v[:, cut])).astype(BF16)
             total = total + dot(hidden, down_v[cut, :])
         y_v[...] = total.astype(BF16)
-        for w, (b, cw) in enumerate(windows):
-            place = (shift_ref[b, 0] - 1) * 32 + shift_ref[b, 1] + OFFSETS[cw]
+        for w, cw in enumerate(columns):
+            place = (s - 1) * 32 + t + OFFSETS[cw]
             at = lax.broadcasted_iota(jnp.int32, (512, SPAN), 0)
             put = jnp.where(at == from_cells_ref[0:1, :] + place, 1.0, 0.0).astype(BF16)
             moved = dot(put, y_v[w * SPAN : (w + 1) * SPAN, :]).astype(BF16).reshape(2, 8, 32, D)
-            where = (slice(2 * b, 2 * b + 2), pl.ds(first_row, 8), slice(BASES[cw], BASES[cw] + 32))
+            where = (levels, pl.ds(first_row, 8), slice(BASES[cw], BASES[cw] + 32))
             result[where] = result[where] + moved
 
     def back(i, source, target, lat, lon):
@@ -337,82 +450,153 @@
             source, target, back_send.at[i], back_recv.at[i], device_id=(lat, lon), device_id_type=MESH
         )
 
-    backs = (
-        back(0, result.at[:, pl.ds(ROWS, HALO), pl.ds(0, COLS), :], from_north, south, lo),
-        back(1, result.at[:, pl.ds(0, ROWS), pl.ds(COLS, GRP), :], from_west, la, east),
-        back(2, result.at[:, pl.ds(ROWS, HALO), pl.ds(COLS, GRP), :], from_corner, south, east),
-    )
-
+    def back_south(i, b, columns):
+        levels = pl.ds(2 * b, 2)
+        return back(
+            i,
+            result.at[levels, pl.ds(ROWS, HALO), pl.ds(*columns), :],
+            from_north.at[levels, :, pl.ds(*columns), :],
+            south,
+            lo,
+        )
+
+    def back_east(i, b, pairs):
+        where = (pl.ds(2 * b, 2), pl.ds(*pairs))
+        return back(i, back_out.at[where], from_west.at[where], la, east)
+
+    def back_corner(i, b):
+        levels = pl.ds(2 * b, 2)
+        return back(i, back_out.at[levels, pl.ds(ROWS // 2, 2)], from_corner.at[levels], south, east)
+
+    def back_pack(b, first, count):
+        levels = slice(2 * b, 2 * b + 2)
+        back_out[levels, first : first + count] = packed(
+            result[levels, 2 * first : 2 * (first + count), COLS : COLS + EDGE, :]
+        )
+
+    first_backs = [back_south(b, b, (0, GRP)) for b in range(2)]
+    souths = [back_south(2 + b, b, (GRP, COLS - GRP)) for b in range(2)]
+    corners = [back_corner(4 + b, b) for b in range(2)]
+    uppers = [back_east(6, 0, (0, 3)), back_east(7, 1, (0, 5))]
+    lowers = [back_east(8, 0, (3, 3)), back_east(9, 1, (5, 1))]
+
+    next_group(0)
     aggregate_group(0)
     loads[7].wait()
+    ahead_out[...] = packed(latent[:, 0:ROWS, 0:EDGE, :])
     row_halos[0].start()
+    corner_halo.start()
     col_halo.start()
-    corner_halo.start()
+    next_group(1)
     aggregate_group(1)
     row_halos[1].start()
     for i in range(3, 7):
         loads[i].wait()
 
-    def first_pair(rw, carry):
-        @pl.when(rw == 1)
-        def _():
+    def first_pair(i, carry):
+        @pl.when(i == 1)
+        def _():
+            send_on(2, True)
+
+        @pl.when(i == 2)
+        def _():
+            send_on(2, False)
             row_halos[0].wait_recv()
             row_halos[1].wait_recv()
 
-        attend(0, rw)
+        attend(0, i // 2, lax.rem(i, 2))
         return carry
 
-    lax.fori_loop(0, 2, first_pair, 0)
+    lax.fori_loop(0, 4, first_pair, 0)
+    for copy in first_backs:
+        copy.start()
     aggregate_group(2)
     row_halos[2].start()
-
-    def second_pair(rw, carry):
-        @pl.when(rw == 0)
-        def _():
-            col_halo.wait_recv()
-
-        @pl.when(rw == 1)
+    row_halos[3].start()
+    col_halo.wait_recv()
+    latent[:, 0:ROWS, COLS : COLS + EDGE, :] = unpacked(ahead_in[...])
+    corner_halo.wait_recv()
+    latent[:, ROWS : ROWS + HALO, COLS : COLS + EDGE, :] = unpacked(ahead_corner[...])[:, :HALO]
+
+    def second_pair(i, carry):
+        b = i // 2
+        rw = lax.rem(i + b, 2)
+
+        @pl.when(i == 1)
         def _():
             row_halos[2].wait_recv()
-            corner_halo.wait_recv()
-
-        attend(1, rw)
+
+        @pl.when(i == 2)
+        def _():
+            row_halos[3].wait_recv()
+
+        attend(1, rw, b)
+
+        @pl.when(i == 0)
+        def _():
+            back_pack(0, 0, 3)
+            uppers[0].start()
+
+        @pl.when(i == 1)
+        def _():
+            souths[0].start()
+            back_pack(0, 3, 5)
+            corners[0].start()
+            lowers[0].start()
+
+        @pl.when(i == 2)
+        def _():
+            souths[1].start()
+            back_pack(1, 5, 3)
+            corners[1].start()
+            lowers[1].start()
+
+        @pl.when(i == 3)
+        def _():
+            back_pack(1, 0, 5)
+            uppers[1].start()
+
         return carry
 
-    lax.fori_loop(0, 2, second_pair, 0)
-    for copy in backs:
-        copy.start()
-    for copy in backs:
-        copy.wait_recv()
-    result[:, 0:HALO, 0:COLS, :] = result[:, 0:HALO, 0:COLS, :] + from_north[...]
-    result[:, 0:ROWS, 0:GRP, :] = result[:, 0:ROWS, 0:GRP, :] + from_west[...]
-    result[:, 0:HALO, 0:GRP, :] = result[:, 0:HALO, 0:GRP, :] + from_corner[...]
-    done = pltpu.make_async_copy(result.at[:, pl.ds(0, ROWS), pl.ds(0, COLS), :], out, out_sem)
-    done.start()
-    for copy in backs:
-        copy.wait_send()
+    lax.fori_loop(0, 4, second_pair, 0)
+    def finished(b):
+        levels = pl.ds(2 * b, 2)
+        return pltpu.make_async_copy(
+            result.at[levels, pl.ds(0, ROWS), pl.ds(0, COLS), :], out.at[levels], out_sem.at[b]
+        )
+
+    for b in range(2):
+        levels = slice(2 * b, 2 * b + 2)
+        for copies in (first_backs, souths, corners, lowers, uppers):
+            copies[b].wait_recv()
+        result[levels, 0:HALO, 0:COLS, :] = result[levels, 0:HALO, 0:COLS, :] + from_north[levels]
+        result[levels, 0:ROWS, 0:EDGE, :] = result[levels, 0:ROWS, 0:EDGE, :] + unpacked(from_west[levels])
+        result[levels, 0:HALO, 0:EDGE, :] = (
+            result[levels, 0:HALO, 0:EDGE, :] + unpacked(from_corner[levels])[:, :HALO]
+        )
+        finished(b).start()
+    for copies in (first_backs, souths, corners, lowers, uppers):
+        for copy in copies:
+            copy.wait_send()
     for copy in row_halos + [col_halo, corner_halo]:
         copy.wait_send()
 
-    def sent(i, carry):
-        g, k = i // lons, lax.rem(i, lons)
-        lon, source, target = part_copy(g, k)
-
-        @pl.when(jnp.logical_not(is_self(dest_lat, lon)))
-        def _():
-            pltpu.make_async_remote_copy(
-                source,
-                target,
-                send_sem.at[g, k],
-                recv_sem.at[g, half, la],
-                device_id=(dest_lat, lon),
-                device_id_type=MESH,
-            ).wait_send()
-
+    def sent(k, carry):
+        sent_part(GROUPS - 1, k)
         return carry
 
-    lax.fori_loop(0, GROUPS * lons, sent, 0)
-    done.wait()
+    lax.fori_loop(0, lons, sent, 0)
+
+    @pl.when(outer)
+    def _():
+        def step(i, carry):
+            relay_copy(i // lats, lax.rem(i, 2), lax.rem(i // 2, half_lats)).wait_send()
+            return carry
+
+        lax.fori_loop(0, GROUPS * lats, step, 0)
+
+    for b in range(2):
+        finished(b).wait()
 
 
 def shards(
@@ -450,11 +634,16 @@
         out_specs=hbm,
         scratch_shapes=[
             pltpu.VMEM((GROUPS, 2, lats, WIN_LAT, GRP, D), BF16),
+            pltpu.VMEM((GROUPS, 2, lats // 2, WIN_LAT, GRP, D), BF16),
             pltpu.VMEM((LATENT, ROWS + HALO, COLS + GRP, D), BF16),
-            pltpu.VMEM((LATENT, ROWS + HALO, COLS + GRP, D), BF16),
+            pltpu.VMEM((LATENT, ROWS + HALO + 1, COLS + GRP, D), BF16),
             pltpu.VMEM((LATENT, HALO, COLS, D), BF16),
-            pltpu.VMEM((LATENT, ROWS, GRP, D), BF16),
-            pltpu.VMEM((LATENT, HALO, GRP, D), BF16),
+            pltpu.VMEM((LATENT, ROWS // 2, GRP, D), BF16),
+            pltpu.VMEM((LATENT, 2, GRP, D), BF16),
+            pltpu.VMEM((LATENT, ROWS // 2, GRP, D), BF16),
+            pltpu.VMEM((LATENT, ROWS // 2, GRP, D), BF16),
+            pltpu.VMEM((LATENT, 2, GRP, D), BF16),
+            pltpu.VMEM((LATENT, ROWS // 2 + 2, GRP, D), BF16),
             pltpu.VMEM((D, D), BF16),
             pltpu.VMEM((D, D), BF16),
             pltpu.VMEM((D, D), BF16),
@@ -478,12 +667,14 @@
             pltpu.VMEM((BATCH, D), BF16),
             pltpu.SemaphoreType.DMA((GROUPS, lons)),
             pltpu.SemaphoreType.DMA((GROUPS, 2, lats)),
+            pltpu.SemaphoreType.DMA((GROUPS, 2, lats // 2)),
+            pltpu.SemaphoreType.DMA((GROUPS, 2, lats // 2)),
             pltpu.SemaphoreType.DMA((8,)),
-            pltpu.SemaphoreType.DMA((GROUPS + 2,)),
-            pltpu.SemaphoreType.DMA((GROUPS + 2,)),
-            pltpu.SemaphoreType.DMA((3,)),
-            pltpu.SemaphoreType.DMA((3,)),
-            pltpu.SemaphoreType.DMA,
+            pltpu.SemaphoreType.DMA((6,)),
+            pltpu.SemaphoreType.DMA((6,)),
+            pltpu.SemaphoreType.DMA((10,)),
+            pltpu.SemaphoreType.DMA((10,)),
+            pltpu.SemaphoreType.DMA((2,)),
         ],
         compiler_params=pltpu.CompilerParams(
             collective_id=0, has_side_effects=True, vmem_limit_bytes=56 * 1024 * 1024

time: 195 us -> 142 us (0.73)
  the two profiles are of different devices: /device:TPU:1 before, /device:TPU:24 now
where the time goes in v2:
time: 142 us
  Pallas kernels  139 us (98%)
  local copies, waits for them, and re-layouts  3.24 us (2%)
    pallas_call x1, Pallas kernels, shards(): pl.pallas_call(functools.partial(kernel, lats, lons), out_shape=jax.Shape...  139 us
    unnamed x1, local copies, waits for them, and re-layouts  3.24 us

profile of v2, /device:TPU:24, one launch (start us, length us, event | category | flops | bytes accessed | tf_op | source)
XLA Modules:
  0.0 142.3 jit_solution(16127840043972422316)
XLA Ops:
  0.0 139.0 %encoder.1 = bf16[4,12,48,512]{3,2,1,0:T(8,128)(2,1)} custom-call(s32[8]{0:T(128)} %order_ref.1, s32[2,2]{1,0:T(2,128)} %shift_ref.1, bf16[1,6,768,512]{3,2,1,0:T(8,128)(2,1)} %slabs.1, bf16[12,48,512]{2,1,0:T(8,128)(2,1)} %surf.1, bf16[8,512]{1,0:T(8,128)(2,1)} %embed_ref.1, f32[1,512]{1,0:T(1,128)} %bitcast.3, bf16[3,512]{1,0:T(4,128)(2,1)} %queries_ref.1, ...), custom_call_target="tpu_custom_call" | custom-call | tf_op jit(solution)/shard_map/encoder/pallas_call | solution.py:630
  139.0 3.2 %copy.20 = bf16[4,12,48,512]{3,2,1,0:T(8,128)(2,1)} copy(bf16[4,12,48,512]{3,2,1,0:T(8,128)(2,1)} %encoder.1) | data formatting | bytes 4718592
